TPU v7x, 128 devices: a whole 4x4x4 slice. The times are simulated.
128 devices in a mesh: gx: 4 (over z), gy: 8 (over x, y_lo), gz: 4 (over y_hi, core).
Axes of the slice: x: 4, y: 4 (y_hi: 2, y_lo: 2; y = y_hi * 2 + y_lo), z: 4, core: 2. Of those that a mesh axis runs over, the one named last changes fastest.
Arguments:
- tokens: bfloat16 [1024, 8192], P('gy', ('gx', 'gz')), may hold values from -6 to 6
- grad_out: bfloat16 [1024, 8192], P('gy', ('gx', 'gz')), may hold values from -6 to 6
- gate_pre: bfloat16 [1024, 14784], P(('gx', 'gz'), 'gy'), may hold values from -8 to 8
- up_pre: bfloat16 [1024, 14784], P(('gx', 'gz'), 'gy'), may hold values from -6 to 6
- gate_weight: bfloat16 [8192, 14784], P(('gx', 'gz'), 'gy'), may hold values from -0.0625 to 0.0625
- up_weight: bfloat16 [8192, 14784], P(('gx', 'gz'), 'gy'), may hold values from -0.0625 to 0.0625
- down_weight: bfloat16 [14784, 8192], P('gy', ('gx', 'gz')), may hold values from -0.046875 to 0.046875
Outputs:
- grad_tokens: bfloat16 [1024, 8192], P('gy', ('gx', 'gz'))
- grad_gate_weight: bfloat16 [8192, 14784], P(('gx', 'gz'), 'gy')
- grad_up_weight: bfloat16 [8192, 14784], P(('gx', 'gz'), 'gy')
- grad_down_weight: bfloat16 [14784, 8192], P('gy', ('gx', 'gz'))
All inputs are finite; a program needn't handle non-finite values.
Results may differ from a plain program's by a relative error of at most 0.027.
Values may be sent and summed in bfloat16 or wider, within the bound.
A program may use at most 128 MiB of HBM per device.

v0:
```python
import math

import jax
import jax.numpy as jnp
from jax import lax
from jax.sharding import PartitionSpec as P


def activation_grads(hidden_grad, gate_pre, up_pre):
    gate_value = gate_pre.astype(jnp.float32)
    up_value = up_pre.astype(jnp.float32)
    sigmoid_gate = jax.nn.sigmoid(gate_value)
    grad_gate_pre = (
        hidden_grad * up_value * sigmoid_gate * (1.0 + gate_value * (1.0 - sigmoid_gate))
    ).astype(jnp.bfloat16)
    grad_up_pre = (hidden_grad * gate_value * sigmoid_gate).astype(jnp.bfloat16)
    hidden = (gate_value * sigmoid_gate * up_value).astype(jnp.bfloat16)
    return (grad_gate_pre, grad_up_pre, hidden)


def contract_last(left, right):
    return lax.dot_general(
        left, right, (((1,), (1,)), ((), ())), preferred_element_type=jnp.float32
    )


def contract_first(left, right):
    return lax.dot_general(
        left, right, (((0,), (0,)), ((), ())), preferred_element_type=jnp.float32
    )


def local(tokens, grad_out, gate_pre, up_pre, gate_weight, up_weight, down_weight):
    inputs_all, upstream = (
        lax.all_gather(tokens, "gy", axis=0, tiled=True),
        lax.all_gather(grad_out, "gy", axis=0, tiled=True),
    )
    shared_rows = lax.psum_scatter(
        contract_last(upstream, down_weight).astype(jnp.bfloat16),
        ("gx", "gz"),
        scatter_dimension=0,
        tiled=True,
    ).astype(jnp.float32)
    local_gate, local_up, local_hidden = activation_grads(shared_rows, gate_pre, up_pre)
    grad_gate_pre, grad_up_pre, hidden = (
        lax.all_gather(local_gate, ("gx", "gz"), axis=0, tiled=True),
        lax.all_gather(local_up, ("gx", "gz"), axis=0, tiled=True),
        lax.all_gather(local_hidden, ("gx", "gz"), axis=0, tiled=True),
    )
    input_term = contract_last(grad_gate_pre, gate_weight) + contract_last(grad_up_pre, up_weight)
    grad_tokens = lax.psum_scatter(
        input_term.astype(jnp.bfloat16), "gy", scatter_dimension=0, tiled=True
    )
    grad_scale = 1.0 / math.sqrt(upstream.shape[0])
    grad_gate_weight = (contract_first(inputs_all, grad_gate_pre) * grad_scale).astype(jnp.bfloat16)
    grad_up_weight = (contract_first(inputs_all, grad_up_pre) * grad_scale).astype(jnp.bfloat16)
    grad_down_weight = (contract_first(hidden, upstream) * grad_scale).astype(jnp.bfloat16)
    return (grad_tokens, grad_gate_weight, grad_up_weight, grad_down_weight)


def solution(mesh):
    return jax.shard_map(
        local,
        mesh=mesh,
        in_specs=(
            P("gy", ("gx", "gz")),
            P("gy", ("gx", "gz")),
            P(("gx", "gz"), "gy"),
            P(("gx", "gz"), "gy"),
            P(("gx", "gz"), "gy"),
            P(("gx", "gz"), "gy"),
            P("gy", ("gx", "gz")),
        ),
        out_specs=(
            P("gy", ("gx", "gz")),
            P(("gx", "gz"), "gy"),
            P(("gx", "gz"), "gy"),
            P("gy", ("gx", "gz")),
        ),
        check_vma=False,
    )
```

profile of v0, /device:TPU:1, one launch (start us, length us, event | category | flops | bytes accessed | tf_op | source)
XLA Modules:
  0.0 385.1 jit_solution(8135717846251595650)
XLA Ops:
  7.2 0.7 all-gather.6.cloned.1.call-update
  7.9 0.0 reduce-scatter.3.cloned.1.call-start
  8.0 39.4 %all-gather.6.cloned.1.call-done = bf16[1024,512]{1,0:T(8,128)(2,1)} async-done(((bf16[128,512]{1,0:T(8,128)(2,1)}), bf16[1024,512]{1,0:T(8,128)(2,1)}) %all-gather.6.cloned.1.call-update) | async-done | bytes 1048592 | tf_op jit(solution)/shard_map/all_gather | solution.py:36
  47.4 5.5 %convolution_convert_fusion = bf16[1024,1848]{1,0:T(8,128)(2,1)} fusion(bf16[1024,512]{1,0:T(8,128)(2,1)} %all-gather.6.cloned.1.call-done, bf16[1848,512]{1,0:T(8,128)(2,1)S(1)} %copy-done), kind=kOutput, calls=%fused_computation.3 | convolution fusion | flops 1939660800 | bytes 6725632 | tf_op jit(solution)/shard_map/dot_general | solution.py:22
  52.9 0.0 all-gather.8.cloned.1.call-start
  52.9 81.5 %reduce-scatter.3.cloned.1.call-done = bf16[64,1848]{1,0:T(8,128)(2,1)} async-done(((bf16[1024,1848]{1,0:T(8,128)(2,1)}), bf16[64,1848]{1,0:T(8,128)(2,1)}) %reduce-scatter.3.cloned.1.call-update) | async-done | bytes 236560 | tf_op jit(solution)/shard_map/reduce_scatter | solution.py:38
  134.4 2.1 fusion.5
  136.5 0.0 all-gather.10.cloned.1.call-start
  136.6 0.5 all-gather.10.cloned.1.call-update
  137.1 0.0 all-gather.12.cloned.1.call-start
  137.2 0.5 all-gather.12.cloned.1.call-update
  137.7 0.0 all-gather.14.cloned.1.call-start
  137.8 0.5 all-gather.14.cloned.1.call-update
  138.3 0.0 reduce-scatter.5.cloned.1.call-start
  138.3 54.1 %all-gather.8.cloned.1.call-done = bf16[1024,1848]{1,0:T(8,128)(2,1)} async-done(((bf16[64,1848]{1,0:T(8,128)(2,1)}), bf16[1024,1848]{1,0:T(8,128)(2,1)}) %all-gather.8.cloned.1.call-update) | async-done | bytes 3784720 | tf_op jit(solution)/shard_map/all_gather | solution.py:46
  192.4 6.4 %fusion.12 = f32[1024,512]{1,0:T(8,128)} fusion(bf16[1024,1848]{1,0:T(8,128)(2,1)} %all-gather.8.cloned.1.call-done, bf16[512,1848]{0,1:T(8,128)(2,1)} %param.11), kind=kOutput, calls=%fused_computation.23 | convolution fusion | flops 1937768448 | bytes 7774208 | tf_op jit(solution)/shard_map/dot_general | solution.py:22
  198.8 48.7 %all-gather.10.cloned.1.call-done = bf16[1024,1848]{1,0:T(8,128)(2,1)} async-done(((bf16[64,1848]{1,0:T(8,128)(2,1)}), bf16[1024,1848]{1,0:T(8,128)(2,1)}) %all-gather.10.cloned.1.call-update) | async-done | bytes 3784720 | tf_op jit(solution)/shard_map/all_gather | solution.py:47
  247.6 6.6 %add_convert_fusion = bf16[1024,512]{1,0:T(8,128)(2,1)} fusion(f32[1024,512]{1,0:T(8,128)} %fusion.12, bf16[1024,1848]{1,0:T(8,128)(2,1)} %all-gather.10.cloned.1.call-done, bf16[512,1848]{0,1:T(8,128)(2,1)} %param.12), kind=kOutput, calls=%fused_computation.6 | convolution fusion | flops 1938817024 | bytes 8822784 | tf_op jit(solution)/shard_map/dot_general | solution.py:22
  254.2 26.8 %all-gather.12.cloned.1.call-done = bf16[1024,512]{1,0:T(8,128)(2,1)} async-done(((bf16[128,512]{1,0:T(8,128)(2,1)}), bf16[1024,512]{1,0:T(8,128)(2,1)}) %all-gather.12.cloned.1.call-update) | async-done | bytes 1048592 | tf_op jit(solution)/shard_map/all_gather | solution.py:35
  281.0 6.0 %fusion = bf16[512,1848]{0,1:T(8,128)(2,1)} fusion(bf16[1024,1848]{1,0:T(8,128)(2,1)} %all-gather.8.cloned.1.call-done, bf16[1024,512]{1,0:T(8,128)(2,1)} %all-gather.12.cloned.1.call-done), kind=kOutput, calls=%fused_computation.4 | convolution fusion | flops 1939660800 | bytes 6725632 | tf_op jit(solution)/shard_map/dot_general | solution.py:28
  287.0 3.4 fusion.1
  290.4 52.4 %all-gather.14.cloned.1.call-done = bf16[1024,1848]{1,0:T(8,128)(2,1)} async-done(((bf16[64,1848]{1,0:T(8,128)(2,1)}), bf16[1024,1848]{1,0:T(8,128)(2,1)}) %all-gather.14.cloned.1.call-update) | async-done | bytes 3784720 | tf_op jit(solution)/shard_map/all_gather | solution.py:48
  342.8 5.5 %multiply_convert_fusion = bf16[1848,512]{1,0:T(8,128)(2,1)} fusion(bf16[1024,1848]{1,0:T(8,128)(2,1)} %all-gather.14.cloned.1.call-done, bf16[1024,512]{1,0:T(8,128)(2,1)S(1)} %copy-done.4), kind=kOutput, calls=%fused_computation | convolution fusion | flops 1939660800 | bytes 6725632 | tf_op jit(solution)/shard_map/dot_general | solution.py:28
  348.3 29.9 %reduce-scatter.5.cloned.1.call-done = bf16[128,512]{1,0:T(8,128)(2,1)} async-done(((bf16[1024,512]{1,0:T(8,128)(2,1)}), bf16[128,512]{1,0:T(8,128)(2,1)}) %reduce-scatter.5.cloned.1.call-update) | async-done | bytes 131088 | tf_op jit(solution)/shard_map/reduce_scatter | solution.py:51
  (16 shorter events, 0.1 us)
Async XLA Ops:
  7.2 40.2 %copy-start = (bf16[1848,512]{1,0:T(8,128)(2,1)S(1)}, bf16[1848,512]{1,0:T(8,128)(2,1)}, u32[]{:S(2)}) copy-start(bf16[1848,512]{1,0:T(8,128)(2,1)} %param.13) | copy-start | bytes 5677060
  7.2 40.2 %all-gather.6.cloned.1.call-start = ((), (), s32[]{:S(2)}) async-start(), calls=%async_computation.2 | async-start | bytes 1179648 | tf_op jit(solution)/shard_map/all_gather | solution.py:36
  7.9 126.5 %reduce-scatter.3.cloned.1.call-start = ((), (), s32[]{:S(2)}) async-start(), calls=%async_computation.3 | async-start | bytes 4177920 | tf_op jit(solution)/shard_map/reduce_scatter | solution.py:38
  52.9 81.6 %copy-start.1 = (bf16[64,1848]{1,0:T(8,128)(2,1)S(1)}, bf16[64,1848]{1,0:T(8,128)(2,1)}, u32[]{:S(2)}) copy-start(bf16[64,1848]{1,0:T(8,128)(2,1)} %param.10) | copy-start | bytes 709636
  52.9 81.6 %copy-start.2 = (bf16[64,1848]{1,0:T(8,128)(2,1)S(1)}, bf16[64,1848]{1,0:T(8,128)(2,1)}, u32[]{:S(2)}) copy-start(bf16[64,1848]{1,0:T(8,128)(2,1)} %param.9) | copy-start | bytes 709636
  52.9 139.5 %all-gather.8.cloned.1.call-start = ((), (), s32[]{:S(2)}) async-start(), calls=%async_computation.4 | async-start | bytes 4177920 | tf_op jit(solution)/shard_map/all_gather | solution.py:46
  136.5 111.0 %all-gather.10.cloned.1.call-start = ((), (), s32[]{:S(2)}) async-start(), calls=%async_computation.5 | async-start | bytes 4177920 | tf_op jit(solution)/shard_map/all_gather | solution.py:47
  137.1 143.9 %all-gather.12.cloned.1.call-start = ((), (), s32[]{:S(2)}) async-start(), calls=%async_computation.7 | async-start | bytes 1179648 | tf_op jit(solution)/shard_map/all_gather | solution.py:35
  137.7 205.1 %all-gather.14.cloned.1.call-start = ((), (), s32[]{:S(2)}) async-start(), calls=%async_computation.8 | async-start | bytes 4177920 | tf_op jit(solution)/shard_map/all_gather | solution.py:48
  138.3 240.0 %reduce-scatter.5.cloned.1.call-start = ((), (), s32[]{:S(2)}) async-start(), calls=%async_computation.6 | async-start | bytes 1179648 | tf_op jit(solution)/shard_map/reduce_scatter | solution.py:51
  281.0 6.0 %copy-start.3 = (bf16[1024,1848]{1,0:T(8,128)(2,1)S(1)}, bf16[1024,1848]{1,0:T(8,128)(2,1)}, u32[]{:S(2)}) copy-start(bf16[1024,1848]{1,0:T(8,128)(2,1)} %all-gather.10.cloned.1.call-done) | copy-start | bytes 11354116
  281.0 6.0 %copy-start.5 = (bf16[1024,512]{1,0:T(8,128)(2,1)S(1)}, bf16[1024,512]{1,0:T(8,128)(2,1)}, u32[]{:S(2)}) copy-start(bf16[1024,512]{1,0:T(8,128)(2,1)} %all-gather.12.cloned.1.call-done) | copy-start | bytes 3145732
  287.0 55.8 %copy-start.4 = (bf16[1024,512]{1,0:T(8,128)(2,1)S(1)}, bf16[1024,512]{1,0:T(8,128)(2,1)}, u32[]{:S(2)}) copy-start(bf16[1024,512]{1,0:T(8,128)(2,1)} %all-gather.6.cloned.1.call-done) | copy-start | bytes 3145732
Sparse Core Ops, SparseCore 0:
  9.7 37.6 all-gather.5
  53.0 81.3 reduce-scatter.2
  137.8 54.5 all-gather.7
  195.6 51.9 all-gather.9
  249.2 31.7 all-gather.11
  284.2 58.5 all-gather.13
  345.9 32.3 reduce-scatter.4
where the time goes:
time: 389 us; the launch traced here: 385 us
  waiting for transfers between devices  335 us (86%)
  matrix products  33.4 us (9%)
  between operations  14.1 us (4%)
    reduce_scatter x1, waiting for transfers between devices, local(): lax.psum_scatter(contract_last(upstream, down_weight).astype(jnp.bfloat16...  81.5 us
    all_gather x1, waiting for transfers between devices, local(): lax.all_gather(local_gate, ('gx', 'gz'), axis=0, tiled=True)  54.1 us
    all_gather x1, waiting for transfers between devices, local(): lax.all_gather(local_hidden, ('gx', 'gz'), axis=0, tiled=True)  52.4 us
    all_gather x1, waiting for transfers between devices, local(): lax.all_gather(local_up, ('gx', 'gz'), axis=0, tiled=True)  48.7 us
    all_gather x1, waiting for transfers between devices, local(): lax.all_gather(grad_out, 'gy', axis=0, tiled=True)  39.4 us
    reduce_scatter x1, waiting for transfers between devices, local(): lax.psum_scatter(input_term.astype(jnp.bfloat16), 'gy', scatter_dimension...  29.9 us
    all_gather x1, waiting for transfers between devices, local(): lax.all_gather(tokens, 'gy', axis=0, tiled=True)  26.8 us
    dot_general x3, matrix products, contract_last(): lax.dot_general(left, right, (((1,), (1,)), ((), ())), preferred_element_...  18.5 us
  transfers between devices with their start and end apart: 7, of which 7 were waited for; matrix products, arithmetic and copies ran while one was open for 7% of the time, Pallas kernels for 0%

commit v1 on v0

v1 whole, which is shorter than its diff:
```python
import functools
import math

import jax
import jax.numpy as jnp
from jax import lax
from jax.experimental import pallas as pl
from jax.experimental.pallas import tpu as pltpu
from jax.sharding import PartitionSpec as P

MESH = pl.DeviceIdType.MESH
F32 = jnp.float32
BF16 = jnp.bfloat16
FB = 1848
DB = 512
LANES = ((0, 512), (512, 1024), (1024, 1536), (1536, 1848))
N_REMOTE = 96
SCALE = 1.0 / 32.0


def nt(a, b):
    return lax.dot_general(a, b, (((1,), (1,)), ((), ())), preferred_element_type=F32)


def tn(a, b):
    return lax.dot_general(a, b, (((0,), (0,)), ((), ())), preferred_element_type=F32)


def kernel(
    tok_in, go_in, gate_in, up_in, wg_in, wu_in, dw_in,
    gt_out, dwg_out, dwu_out, dwd_out,
    gu, hg, ab, hid, go, tok, gos, dw, dws, wg, wu, part, r1, s1, r2, r3, q1, r4,
    gt, rg, tokt, og, ou, od, ot, ss, rs, ls,
):
    z = lax.axis_index("gx")
    gy = lax.axis_index("gy")
    gz = lax.axis_index("gz")
    x, l = gy // 2, gy % 2
    h, c = gz // 2, gz % 2
    nc, nh = 1 - c, 1 - h
    other_gy = x * 2 + (1 - l)
    zs = [lax.rem(z + d, 4) for d in range(4)]

    def zdev(d):
        return (zs[d], gy, gz)

    hidev = (z, gy, nh * 2 + c)
    sib = (z, gy, h * 2 + nc)

    def gydev(dx, dl):
        return (z, lax.rem(x + dx, 4) * 2 + lax.rem(l + dl, 2), gz)

    gy_offsets = [(dx, dl) for dx in range(4) for dl in range(2)][1:]

    sent = []

    def send(src, dst, dev):
        i = len(sent)
        copy = pltpu.make_async_remote_copy(
            src_ref=src, dst_ref=dst, send_sem=ss.at[i], recv_sem=rs.at[i],
            device_id=dev, device_id_type=MESH,
        )
        copy.start()
        sent.append(copy)
        return copy

    def same(ref, dev):
        return send(ref, ref, dev)

    n_local = [0]

    def local(src, dst):
        copy = pltpu.make_async_copy(src, dst, ls.at[n_local[0]])
        n_local[0] += 1
        copy.start()
        return copy

    l_go = local(go_in, go.at[:, :, gy])
    l_gate = local(gate_in, gu.at[0, c, :, z, h])
    l_up = local(up_in, gu.at[1, c, :, z, h])
    l_dw = local(dw_in, dw)
    l_tok = local(tok_in, tok.at[:, :, gy])
    l_wg = local(wg_in, wg)
    l_wu = local(wu_in, wu)

    peers = [sib, hidev] + [zdev(d) for d in (1, 2, 3)] + [gydev(*o) for o in gy_offsets]
    barrier = pltpu.get_barrier_semaphore()
    for dev in peers:
        pl.semaphore_signal(barrier, inc=1, device_id=dev, device_id_type=MESH)
    pl.semaphore_wait(barrier, len(peers))

    l_go.wait()
    go_lo = same(go.at[:, :, gy], gydev(0, 1))
    go_x = [same(go.at[:, :, gy], gydev(d, 0)) for d in (1, 2, 3)]
    l_dw.wait()
    c_dws = send(dw, dws, sib)
    l_gate.wait()
    l_up.wait()
    gu0_hi = same(gu.at[:, c, 0, z, h], hidev)
    gu1_z = [same(gu.at[:, c, 1, z, h], zdev(d)) for d in (1, 2, 3)]
    gu1_hi = [same(gu.at[:, c, 1, z, h], hidev)]

    go_lo.wait_recv()
    go_x2 = [same(go.at[:, :, other_gy], gydev(d, 0)) for d in (1, 2, 3)]
    gu0_hi.wait_recv()
    gu0_z = [same(gu.at[:, c, 0, z], zdev(d)) for d in (1, 2, 3)]

    for copy in go_x + go_x2:
        copy.wait_recv()
    gos_k = [send(go.at[nc, k], gos.at[k], sib) for k in (0, 1)]
    l_tok.wait()
    tok_lo = same(tok.at[:, :, gy], gydev(0, 1))
    tok_x = [same(tok.at[:, :, gy], gydev(d, 0)) for d in (1, 2, 3)]
    c_dws.wait_recv()

    def product(k):
        gos_k[k].wait_recv()
        own = go[c, k].reshape(256, DB)
        other = gos[k].reshape(256, DB)
        for a, b in LANES:
            p = nt(own, dw[a:b, :]) + nt(other, dws[a:b, :])
            part[k, :, :, :, a:b] = p.astype(BF16).reshape(4, 2, 32, b - a)

    product(0)
    rs0_z = [send(part.at[0, zs[d]], r1.at[d - 1], zdev(d)) for d in (1, 2, 3)]
    product(1)
    rs1_hi = send(part.at[1, :, nh], r3, hidev)

    for d in (1, 2, 3):
        gu1_z[d - 1].wait_recv()
        gu1_hi.append(same(gu.at[:, c, 1, zs[4 - d], h], hidev))
    gu1_s = same(gu.at[:, c, 1, :, h], sib)
    tok_lo.wait_recv()
    tok_x2 = [same(tok.at[:, :, other_gy], gydev(d, 0)) for d in (1, 2, 3)]

    rs1_hi.wait_recv()
    for i in range(4):
        for a, b in LANES:
            q1[i, :, a:b] = (part[1, i, h, :, a:b].astype(F32) + r3[i, :, a:b].astype(F32)).astype(BF16)
    rs1_z = [send(q1.at[zs[d]], r4.at[d - 1], zdev(d)) for d in (1, 2, 3)]

    for copy in rs0_z:
        copy.wait_recv()
    for i in range(2):
        for a, b in LANES:
            total = part[0, z, i, :, a:b].astype(F32)
            for d in range(3):
                total = total + r1[d, i, :, a:b].astype(F32)
            s1[i, :, a:b] = total.astype(BF16)
    rs0_hi = send(s1.at[nh], r2, hidev)

    def pointwise(cc, k):
        def block(i, carry):
            zz, hh = i // 2, i % 2
            for a, b in LANES:
                gate = gu[0, cc, k, zz, hh, :, a:b].astype(F32)
                up = gu[1, cc, k, zz, hh, :, a:b].astype(F32)
                s = 0.5 + 0.5 * jnp.tanh(0.5 * gate)
                silu = gate * s
                ab[0, cc, k, zz, hh, :, a:b] = (up * (s * (1.0 + gate - silu))).astype(BF16)
                ab[1, cc, k, zz, hh, :, a:b] = silu.astype(BF16)
                hid[cc, k, zz, hh, :, a:b] = (silu * up).astype(BF16)
            return carry

        lax.fori_loop(0, 8, block, 0)

    for copy in gu0_z:
        copy.wait_recv()
    gu0_s = same(gu.at[:, c, 0], sib)
    pointwise(c, 0)

    for copy in rs1_z:
        copy.wait_recv()
    for a, b in LANES:
        total = q1[z, :, a:b].astype(F32)
        for d in range(3):
            total = total + r4[d, :, a:b].astype(F32)
        hg[c, 1, z, h, :, a:b] = total.astype(BF16)
    hg1_z = [same(hg.at[c, 1, z, h], zdev(d)) for d in (1, 2, 3)]
    hg1_hi = [same(hg.at[c, 1, z, h], hidev)]

    rs0_hi.wait_recv()
    for a, b in LANES:
        total = s1[h, :, a:b].astype(F32) + r2[:, a:b].astype(F32)
        hg[c, 0, z, h, :, a:b] = total.astype(BF16)
    hg0_hi = same(hg.at[c, 0, z, h], hidev)

    for copy in gu1_hi:
        copy.wait_recv()
    gu1_s2 = same(gu.at[:, c, 1, :, nh], sib)
    pointwise(c, 1)

    hg0_hi.wait_recv()
    hg0_z = [same(hg.at[c, 0, z], zdev(d)) for d in (1, 2, 3)]
    hg0_s = [same(hg.at[c, 0, z], sib)]
    for d in (1, 2, 3):
        hg1_z[d - 1].wait_recv()
        hg1_hi.append(same(hg.at[c, 1, zs[4 - d], h], hidev))
    hg1_s = [same(hg.at[c, 1, :, h], sib)]

    gu0_s.wait_recv()
    pointwise(nc, 0)
    gu1_s.wait_recv()
    gu1_s2.wait_recv()
    pointwise(nc, 1)

    stores = []
    for a, b in LANES:
        w = tn(hid[:, :, :, :, :, a:b].reshape(1024, b - a), go[...].reshape(1024, DB))
        od[a:b, :] = (w * SCALE).astype(BF16)
    stores.append(local(od, dwd_out))

    for copy in tok_x + tok_x2:
        copy.wait_recv()
    for cc in range(2):
        for k in range(2):
            i = (cc * 2 + k) * 256
            tokt[:, i : i + 256] = tok[cc, k].reshape(256, DB).T

    l_wg.wait()
    l_wu.wait()

    def input_grad(cc, k):
        def block(i, carry):
            zz, hh = i // 2, i % 2
            for a, b in LANES:
                grad = hg[cc, k, zz, hh, :, a:b]
                ab[0, cc, k, zz, hh, :, a:b] = ab[0, cc, k, zz, hh, :, a:b] * grad
                ab[1, cc, k, zz, hh, :, a:b] = ab[1, cc, k, zz, hh, :, a:b] * grad
            return carry

        lax.fori_loop(0, 8, block, 0)
        term = nt(ab[0, cc, k].reshape(256, FB), wg[...]) + nt(ab[1, cc, k].reshape(256, FB), wu[...])
        gt[cc, k] = term.astype(BF16).reshape(8, 32, DB)

    def send_input_grad(k):
        return [
            send(gt.at[:, k, lax.rem(x + dx, 4) * 2 + lax.rem(l + dl, 2)], rg.at[k, j], gydev(dx, dl))
            for j, (dx, dl) in enumerate(gy_offsets)
        ]

    for d in (1, 2, 3):
        hg0_z[d - 1].wait_recv()
        hg0_s.append(same(hg.at[c, 0, zs[4 - d]], sib))
    input_grad(c, 0)
    for copy in hg0_s:
        copy.wait_recv()
    input_grad(nc, 0)
    gt0 = send_input_grad(0)

    for copy in hg1_hi:
        copy.wait_recv()
    hg1_s.append(same(hg.at[c, 1, :, nh], sib))
    input_grad(c, 1)
    for copy in hg1_s:
        copy.wait_recv()
    input_grad(nc, 1)
    gt1 = send_input_grad(1)

    for which, (out, dst) in enumerate(((og, dwg_out), (ou, dwu_out))):
        for a, b in LANES:
            grads = ab[which, :, :, :, :, :, a:b].reshape(1024, b - a)
            w = jnp.dot(tokt[...], grads, preferred_element_type=F32)
            out[:, a:b] = (w * SCALE).astype(BF16)
        stores.append(local(out, dst))

    for k, copies in enumerate((gt0, gt1)):
        for copy in copies:
            copy.wait_recv()
        for cc in range(2):
            total = gt[cc, k, gy].astype(F32)
            for j in range(7):
                total = total + rg[k, j, cc].astype(F32)
            ot[cc, k] = total.astype(BF16)
    stores.append(local(ot, gt_out))

    for copy in sent:
        copy.wait_send()
    for copy in stores:
        copy.wait()
    assert len(sent) <= N_REMOTE


def local_step(tokens, grad_out, gate_pre, up_pre, gate_weight, up_weight, down_weight):
    any_spec = pl.BlockSpec(memory_space=pl.ANY)
    vm = pltpu.VMEM
    outs = pl.pallas_call(
        kernel,
        out_shape=(
            jax.ShapeDtypeStruct((2, 2, 32, DB), BF16),
            jax.ShapeDtypeStruct((DB, FB), BF16),
            jax.ShapeDtypeStruct((DB, FB), BF16),
            jax.ShapeDtypeStruct((FB, DB), BF16),
        ),
        in_specs=[any_spec] * 7,
        out_specs=(any_spec,) * 4,
        scratch_shapes=[
            vm((2, 2, 2, 4, 2, 32, FB), BF16),
            vm((2, 2, 4, 2, 32, FB), BF16),
            vm((2, 2, 2, 4, 2, 32, FB), BF16),
            vm((2, 2, 4, 2, 32, FB), BF16),
            vm((2, 2, 8, 32, DB), BF16),
            vm((2, 2, 8, 32, DB), BF16),
            vm((2, 8, 32, DB), BF16),
            vm((FB, DB), BF16),
            vm((FB, DB), BF16),
            vm((DB, FB), BF16),
            vm((DB, FB), BF16),
            vm((2, 4, 2, 32, FB), BF16),
            vm((3, 2, 32, FB), BF16),
            vm((2, 32, FB), BF16),
            vm((32, FB), BF16),
            vm((4, 32, FB), BF16),
            vm((4, 32, FB), BF16),
            vm((3, 32, FB), BF16),
            vm((2, 2, 8, 32, DB), BF16),
            vm((2, 7, 2, 32, DB), BF16),
            vm((DB, 1024), BF16),
            vm((DB, FB), BF16),
            vm((DB, FB), BF16),
            vm((FB, DB), BF16),
            vm((2, 2, 32, DB), BF16),
            pltpu.SemaphoreType.DMA((N_REMOTE,)),
            pltpu.SemaphoreType.DMA((N_REMOTE,)),
            pltpu.SemaphoreType.DMA((16,)),
        ],
        compiler_params=pltpu.CompilerParams(
            collective_id=0, has_side_effects=True, vmem_limit_bytes=60 * 1024 * 1024
        ),
        name="swiglu_backward",
    )(
        tokens.reshape(2, 2, 32, DB),
        grad_out.reshape(2, 2, 32, DB),
        gate_pre.reshape(2, 32, FB),
        up_pre.reshape(2, 32, FB),
        gate_weight,
        up_weight,
        down_weight,
    )
    return (outs[0].reshape(128, DB), outs[1], outs[2], outs[3])


def solution(mesh):
    return jax.shard_map(
        local_step,
        mesh=mesh,
        in_specs=(
            P("gy", ("gx", "gz")),
            P("gy", ("gx", "gz")),
            P(("gx", "gz"), "gy"),
            P(("gx", "gz"), "gy"),
            P(("gx", "gz"), "gy"),
            P(("gx", "gz"), "gy"),
            P("gy", ("gx", "gz")),
        ),
        out_specs=(
            P("gy", ("gx", "gz")),
            P(("gx", "gz"), "gy"),
            P(("gx", "gz"), "gy"),
            P("gy", ("gx", "gz")),
        ),
        check_vma=False,
    )
```

time: 389 us -> 115 us (0.30)
  waiting for transfers between devices: 335 us -> 0 us
  Pallas kernels: 0 us -> 97.4 us
  matrix products: 33.4 us -> 0 us
  local copies, waits for them, and re-layouts: 0.03 us -> 16.5 us
  between operations: 14.1 us -> 0.66 us
    all_gather x5 -> x0, waiting for transfers between devices: 221 us -> none  [the longest x1 54.1 us: local(): lax.all_gather(local_gate, ('gx', 'gz'), axis=0, tiled=True)]
    reduce_scatter x2 -> x0, waiting for transfers between devices: 111 us -> none  [the longest x1 81.5 us: local(): lax.psum_scatter(contract_last(upstream, down_weight).astype(jnp.bfloat16...]
    pallas_call x0 -> x1, Pallas kernels: none -> 97.4 us  [local_step(): pl.pallas_call(kernel, out_shape=(jax.ShapeDtypeStruct((2, 2, 32, DB), BF...]
    dot_general x6 -> x0, matrix products: 33.4 us -> none  [the longest x3 18.5 us: contract_last(): lax.dot_general(left, right, (((1,), (1,)), ((), ())), preferred_element_...]
    unnamed x12, local copies, waits for them, and re-layouts: 0.03 us -> 16.5 us
  transfers between devices with their start and end apart: 7 -> 0, of which waited for: 7 -> 0; matrix products, arithmetic and copies ran while one was open for 7% -> 0% of each run, Pallas kernels for 0% -> 0%
where the time goes in v1:
time: 115 us
  Pallas kernels  97.4 us (85%)
  local copies, waits for them, and re-layouts  16.5 us (14%)
    pallas_call x1, Pallas kernels, local_step(): pl.pallas_call(kernel, out_shape=(jax.ShapeDtypeStruct((2, 2, 32, DB), BF...  97.4 us
    unnamed x12, local copies, waits for them, and re-layouts  16.5 us

profile of v1, /device:TPU:1, one launch (start us, length us, event | category | flops | bytes accessed | tf_op | source)
XLA Modules:
  0.0 114.5 jit_solution(7977576484892071104)
XLA Ops:
  0.6 0.0 copy-start.1
  0.6 4.1 %copy.11.wg_in = bf16[512,1848]{1,0:T(8,128)(2,1)} copy(bf16[512,1848]{0,1:T(8,128)(2,1)} %param.11) | data formatting | bytes 3784704 | tf_op args[4]
  4.7 0.0 copy-done.1
  4.7 2.5 %copy.12.wu_in = bf16[512,1848]{1,0:T(8,128)(2,1)} copy(bf16[512,1848]{0,1:T(8,128)(2,1)S(1)} %copy-done.1) | data formatting | bytes 3784704 | tf_op args[5]
  7.2 97.4 %swiglu_backward.1 = (bf16[2,2,32,512]{3,2,1,0:T(8,128)(2,1)}, bf16[512,1848]{1,0:T(8,128)(2,1)}, bf16[512,1848]{1,0:T(8,128)(2,1)}, bf16[1848,512]{1,0:T(8,128)(2,1)}) custom-call(bf16[2,2,32,512]{3,2,1,0:T(8,128)(2,1)} %bitcast.7, bf16[2,2,32,512]{3,2,1,0:T(8,128)(2,1)} %bitcast.8, bf16[2,32,1848]{2,1,0:T(8,128)(2,1)} %bitcast.5, ...), custom_call_target="tpu_custom_call" | custom-call | tf_op jit(solution)/shard_map/swiglu_backward/pallas_call | solution.py:287
  104.6 0.0 copy-start
  104.6 4.1 %copy.13 = bf16[512,1848]{0,1:T(8,128)(2,1)} copy(bf16[512,1848]{1,0:T(8,128)(2,1)} %get-tuple-element.13) | data formatting | bytes 3784704
  108.7 0.0 copy-done
  108.7 0.0 copy-start.2
  108.7 2.3 %copy.14 = bf16[512,1848]{0,1:T(8,128)(2,1)} copy(bf16[512,1848]{1,0:T(8,128)(2,1)S(1)} %copy-done) | data formatting | bytes 3784704
  111.0 0.0 copy-done.2
  111.0 0.7 copy.17
  111.7 2.9 %copy.18 = bf16[1848,512]{1,0:T(8,128)(2,1)} copy(bf16[1848,512]{1,0:T(8,128)(2,1)} %get-tuple-element.23) | data formatting | bytes 3784704
Async XLA Ops:
  0.6 4.1 %copy-start.1 = (bf16[512,1848]{0,1:T(8,128)(2,1)S(1)}, bf16[512,1848]{0,1:T(8,128)(2,1)}, u32[]{:S(2)}) copy-start(bf16[512,1848]{0,1:T(8,128)(2,1)} %param.12) | copy-start | bytes 5677060
  104.6 4.1 %copy-start = (bf16[512,1848]{1,0:T(8,128)(2,1)S(1)}, bf16[512,1848]{1,0:T(8,128)(2,1)}, u32[]{:S(2)}) copy-start(bf16[512,1848]{1,0:T(8,128)(2,1)} %get-tuple-element.14) | copy-start | bytes 5677060
  108.7 2.3 %copy-start.2 = (bf16[2,2,32,512]{3,2,1,0:T(8,128)(2,1)S(1)}, bf16[2,2,32,512]{3,2,1,0:T(8,128)(2,1)}, u32[]{:S(2)}) copy-start(bf16[2,2,32,512]{3,2,1,0:T(8,128)(2,1)} %get-tuple-element.8) | copy-start | bytes 393220

commit v2 on v1

v2 whole, which is shorter than its diff:
```python
import functools
import math

import jax
import jax.numpy as jnp
from jax import lax
from jax.experimental import pallas as pl
from jax.experimental.pallas import tpu as pltpu
from jax.sharding import PartitionSpec as P

MESH = pl.DeviceIdType.MESH
F32 = jnp.float32
BF16 = jnp.bfloat16
FB = 1848
DB = 512
LANES = ((0, 512), (512, 1024), (1024, 1536), (1536, 1848))
N_REMOTE = 112
CHIPS = ((1, 0), (3, 0), (0, 1), (2, 0), (1, 1), (3, 1), (2, 1))
ORDER = ((0, "y"), (1, "z"), (3, "y"), (2, "z"))
SCALE = 1.0 / 32.0


def nt(a, b):
    return lax.dot_general(a, b, (((1,), (1,)), ((), ())), preferred_element_type=F32)


def nn(a, b):
    return lax.dot_general(a, b, (((1,), (0,)), ((), ())), preferred_element_type=F32)


def tn(a, b):
    return lax.dot_general(a, b, (((0,), (0,)), ((), ())), preferred_element_type=F32)


def kernel(
    tok_in, go_in, gate_in, up_in, wg_in, wu_in, dw_in,
    ot, dwg_out, ou, dwd_out,
    gu, hg, ab, hid, go, tok, gos, dw, dws, wg, wu, part, r1, s1, r2, r3, q1, r4, r5,
    gt, rgx, rgd, sl, rl, og, od, ss, rs, ls,
):
    z = lax.axis_index("gx")
    gy = lax.axis_index("gy")
    gz = lax.axis_index("gz")
    x, l = gy // 2, gy % 2
    h, c = gz // 2, gz % 2
    nc, nh = 1 - c, 1 - h
    other_gy = x * 2 + (1 - l)
    zs = [lax.rem(z + d, 4) for d in range(4)]

    def zdev(d):
        return (zs[d], gy, gz)

    hidev = (z, gy, nh * 2 + c)
    sib = (z, gy, h * 2 + nc)

    def chip(e, f):
        return (zs[e], gy, (nh if f else h) * 2 + c)

    def gydev(dx, dl):
        return (z, lax.rem(x + dx, 4) * 2 + lax.rem(l + dl, 2), gz)

    gy_offsets = [(dx, dl) for dx in range(4) for dl in range(2)][1:]

    sent = []

    def remote(src, dst, dev, i):
        return pltpu.make_async_remote_copy(
            src_ref=src, dst_ref=dst, send_sem=ss.at[i], recv_sem=rs.at[i],
            device_id=dev, device_id_type=MESH,
        )

    def send(src, dst, dev):
        copy = remote(src, dst, dev, len(sent))
        copy.start()
        sent.append(copy)
        return copy

    def same(ref, dev):
        return send(ref, ref, dev)

    n_local = [0]

    def local(src, dst):
        copy = pltpu.make_async_copy(src, dst, ls.at[n_local[0]])
        n_local[0] += 1
        copy.start()
        return copy

    l_go = local(go_in, go.at[:, :, gy])
    l_gate = local(gate_in, gu.at[0, c, :, z, h])
    l_up = local(up_in, gu.at[1, c, :, z, h])
    l_dw = local(dw_in, dw)
    l_tok = local(tok_in, tok.at[:, :, gy])
    l_wg = local(wg_in, wg)
    l_wu = local(wu_in, wu)

    peers = [sib, hidev] + [zdev(d) for d in (1, 2, 3)] + [gydev(*o) for o in gy_offsets]
    barrier = pltpu.get_barrier_semaphore()
    for dev in peers:
        pl.semaphore_signal(barrier, inc=1, device_id=dev, device_id_type=MESH)
    pl.semaphore_wait(barrier, len(peers))

    l_go.wait()
    go_lo = same(go.at[:, :, gy], gydev(0, 1))
    go_own = {d: same(go.at[:, :, gy], gydev(d, 0)) for d in (1, 3, 2)}
    l_dw.wait()
    c_dws = send(dw, dws, sib)
    l_gate.wait()
    l_up.wait()
    gu1_z = [same(gu.at[:, c, 1, z, h], zdev(d)) for d in (1, 3)]
    gu0_hi = same(gu.at[:, c, 0, z, h], hidev)
    gu1_hi = [same(gu.at[:, c, 1, z, h], hidev)]
    go_lo.wait_recv()
    go_other = {d: same(go.at[:, :, other_gy], gydev(d, 0)) for d in (1, 3, 2)}

    xts = {d: lax.rem(x + (4 - d), 4) for d in range(4)}
    kind = dict(ORDER)
    slot = {d: [e for e, t in ORDER if t == kind[d]].index(d) for d in kind}
    zk, zh = [v // 2 for v in zs], [v % 2 for v in zs]
    mine = pl.ds(pl.multiple_of(h * 16, 16), 16)
    theirs = pl.ds(pl.multiple_of(nh * 16, 16), 16)
    one, two, spread_one, spread_two, to_sib, gt_copies, gt_last = {}, {}, {}, {}, {}, [], []

    def product(d):
        xt = xts[d]
        pair = pl.ds(xt * 2, 2)
        if d:
            go_own[d].wait_recv()
            go_other[d].wait_recv()
        gos_d = send(go.at[nc, :, pair], gos.at[:, pair], sib)
        if not d:
            c_dws.wait_recv()
        gos_d.wait_recv()
        own = go[c, :, pair].reshape(128, DB)
        other = gos[:, pair].reshape(128, DB)
        for a, b in LANES:
            p = nt(own, dw[a:b, :]) + nt(other, dws[a:b, :])
            part[xt, :, :, :, a:b] = p.astype(BF16).reshape(2, 2, 32, b - a)
        if kind[d] == "z":
            one[d] = [send(part.at[xt, zk[e], zh[e]], r1.at[slot[d], e - 1], zdev(e)) for e in (1, 3, 2)]
        elif kind[d] == "d":
            one[d] = [
                send(part.at[xt, zk[e], zh[e], (mine, theirs)[f]], r5.at[slot[d], j], chip(e, f))
                for j, (e, f) in enumerate(CHIPS)
            ]
        else:
            one[d] = [send(part.at[xt, :, :, theirs], r3.at[slot[d]], hidev)]

    def middle(d):
        xt, i = xts[d], slot[d]
        if kind[d] == "d":
            return
        for copy in one[d]:
            copy.wait_recv()
        if kind[d] == "z":
            for a, b in LANES:
                total = part[xt, zk[0], zh[0], :, a:b].astype(F32)
                for e in range(3):
                    total = total + r1[i, e, :, a:b].astype(F32)
                s1[i, :, a:b] = total.astype(BF16)
            two[d] = [send(s1.at[i, theirs], r2.at[i], hidev)]
        else:
            for a, b in LANES:
                total = part[xt, :, :, mine, a:b].astype(F32) + r3[i, :, :, :, a:b].astype(F32)
                q1[i, :, :, :, a:b] = total.astype(BF16)
            two[d] = [send(q1.at[i, zk[e], zh[e]], r4.at[i, e - 1], zdev(e)) for e in (1, 3, 2)]

    def own_sum(d):
        xt, i = xts[d], slot[d]
        for copy in one[d] if kind[d] == "d" else two[d]:
            copy.wait_recv()
        for a, b in LANES:
            if kind[d] == "z":
                total = s1[i, mine, a:b].astype(F32) + r2[i, :, a:b].astype(F32)
            elif kind[d] == "d":
                total = part[xt, zk[0], zh[0], mine, a:b].astype(F32)
                for j in range(7):
                    total = total + r5[i, j, :, a:b].astype(F32)
            else:
                total = q1[i, zk[0], zh[0], :, a:b].astype(F32)
                for e in range(3):
                    total = total + r4[i, e, :, a:b].astype(F32)
            hg[c, zk[0], xt, zh[0], mine, a:b] = total.astype(BF16)
        block = hg.at[c, zk[0], xt, zh[0], mine]
        if kind[d] == "z":
            spread_one[d] = [same(block, hidev)]
        elif kind[d] == "d":
            spread_one[d] = [same(block, chip(e, f)) for e, f in CHIPS]
        else:
            spread_one[d] = [same(block, zdev(e)) for e in (1, 2, 3)]
            spread_two[d] = [same(block, hidev)]

    def spread(d):
        xt = xts[d]
        if kind[d] == "d":
            return
        if kind[d] == "z":
            spread_one[d][0].wait_recv()
            pair = hg.at[c, zk[0], xt, zh[0]]
            spread_two[d] = [same(pair, zdev(e)) for e in (1, 2, 3)]
            to_sib[d] = [same(pair, sib)]
        else:
            for e in (1, 2, 3):
                spread_one[d][e - 1].wait_recv()
                spread_two[d].append(same(hg.at[c, zk[4 - e], xt, zh[4 - e], mine], hidev))
            to_sib[d] = [same(hg.at[c, :, xt, :, mine], sib)]

    def last_spread(d):
        xt = xts[d]
        if kind[d] == "z":
            for e in (1, 2, 3):
                spread_two[d][e - 1].wait_recv()
                to_sib[d].append(same(hg.at[c, zk[4 - e], xt, zh[4 - e]], sib))
        elif kind[d] == "d":
            for copy in spread_one[d]:
                copy.wait_recv()
            to_sib[d] = [same(hg.at[c, :, xt], sib)]
        else:
            for copy in spread_two[d]:
                copy.wait_recv()
            to_sib[d].append(same(hg.at[c, :, xt, :, theirs], sib))

    def input_grad(d):
        xt = xts[d]
        for copy in to_sib[d]:
            copy.wait_recv()

        def block(i, carry):
            cc, k, hh = i // 4, (i // 2) % 2, i % 2
            for a, b in LANES:
                grad = hg[cc, k, xt, hh, :, a:b]
                ab[0, cc, k, xt, hh, :, a:b] = ab[0, cc, k, xt, hh, :, a:b] * grad
                ab[1, cc, k, xt, hh, :, a:b] = ab[1, cc, k, xt, hh, :, a:b] * grad
            return carry

        lax.fori_loop(0, 8, block, 0)
        term = nn(ab[0, :, :, xt].reshape(256, FB), wg[...])
        term = term + nn(ab[1, :, :, xt].reshape(256, FB), wu[...])
        term = term.astype(BF16).reshape(2, 2, 2, 32, DB)
        for hh in range(2):
            gt[xt, hh] = term[:, :, hh]
        if d == ORDER[-1][0]:
            gt_last.append(send(gt.at[xt, l], rgd.at[0], (z, xt * 2 + l, gz)))
            gt_last.append(send(gt.at[xt, 1 - l], rgd.at[1], (z, xt * 2 + 1 - l, gz)))
        elif d:
            gt_copies.append(send(gt.at[xt], rgx.at[len(gt_copies)], (z, xt * 2 + l, gz)))

    def pointwise(cc, k):
        def block(i, carry):
            zz, hh = i // 2, i % 2
            for a, b in LANES:
                gate = gu[0, cc, k, zz, hh, :, a:b].astype(F32)
                up = gu[1, cc, k, zz, hh, :, a:b].astype(F32)
                s = 0.5 + 0.5 * jnp.tanh(0.5 * gate)
                silu = gate * s
                ab[0, cc, k, zz, hh, :, a:b] = (up * (s * (1.0 + gate - silu))).astype(BF16)
                ab[1, cc, k, zz, hh, :, a:b] = silu.astype(BF16)
                hid[cc, k, zz, hh, :, a:b] = (silu * up).astype(BF16)
            return carry

        lax.fori_loop(0, 8, block, 0)

    d0, d1, d2, d3 = [d for d, _ in ORDER]
    product(d0)
    gu1_z[0].wait_recv()
    gu1_f = [same(gu.at[0, c, 1, zs[3], h], zdev(1))]
    gu1_z[1].wait_recv()
    gu1_f.append(same(gu.at[1, c, 1, zs[1], h], zdev(3)))
    gu0_hi.wait_recv()
    gu0_z = [same(gu.at[:, c, 0, z], zdev(d)) for d in (1, 3)]
    product(d1)
    gu1_hi += [same(gu.at[:, c, 1, zs[d], h], hidev) for d in (1, 3)]
    product(d2)
    middle(d0)
    product(d3)
    middle(d1)
    l_tok.wait()
    tok_lo = same(tok.at[:, :, gy], gydev(0, 1))
    tok_x = [same(tok.at[:, :, gy], gydev(d, 0)) for d in (1, 2, 3)]
    own_sum(d0)
    middle(d2)
    for copy in gu1_f:
        copy.wait_recv()
    gu1_hi.append(same(gu.at[:, c, 1, zs[2], h], hidev))
    gu1_s = same(gu.at[:, c, 1, :, h], sib)
    own_sum(d1)
    spread(d0)
    middle(d3)
    gu0_z[0].wait_recv()
    gu0_f = [same(gu.at[0, c, 0, zs[3]], zdev(1))]
    gu0_z[1].wait_recv()
    gu0_f.append(same(gu.at[1, c, 0, zs[1]], zdev(3)))
    own_sum(d2)
    spread(d1)
    tok_lo.wait_recv()
    tok_x2 = [same(tok.at[:, :, other_gy], gydev(d, 0)) for d in (1, 2, 3)]
    last_spread(d0)
    own_sum(d3)
    spread(d2)
    for copy in gu1_hi:
        copy.wait_recv()
    gu1_s2 = same(gu.at[:, c, 1, :, nh], sib)
    pointwise(c, 1)
    last_spread(d1)
    spread(d3)
    for copy in gu0_f:
        copy.wait_recv()
    gu0_s = same(gu.at[:, c, 0], sib)
    pointwise(c, 0)
    gu1_s.wait_recv()
    gu1_s2.wait_recv()
    pointwise(nc, 1)
    last_spread(d2)
    gu0_s.wait_recv()
    pointwise(nc, 0)
    l_wg.wait()
    l_wu.wait()
    input_grad(d0)
    last_spread(d3)
    input_grad(d1)
    input_grad(d2)
    input_grad(d3)
    for copy in gt_copies:
        copy.wait_recv()
    for cc in range(2):
        total = gt[x, 1 - l, cc].astype(F32) + rgx[0, 1 - l, cc].astype(F32) + rgx[1, 1 - l, cc].astype(F32)
        sl[cc] = total.astype(BF16)
    gt_last.append(send(sl, rl, gydev(0, 1)))
    for copy in tok_x + tok_x2:
        copy.wait_recv()
    stores = []
    for a, b in LANES:
        w = tn(hid[:, :, :, :, :, a:b].reshape(1024, b - a), go[...].reshape(1024, DB))
        od[a:b, :] = (w * SCALE).astype(BF16)
    stores.append(local(od, dwd_out))
    for which, out in enumerate((og, ou)):
        for a, b in LANES:
            grads = ab[which, :, :, :, :, :, a:b].reshape(1024, b - a)
            w = tn(grads, tok[...].reshape(1024, DB))
            out[a:b, :] = (w * SCALE).astype(BF16)
        if which == 0:
            stores.append(local(og, dwg_out))

    for copy in gt_last:
        copy.wait_recv()
    for cc in range(2):
        total = gt[x, l, cc].astype(F32) + rl[cc].astype(F32)
        for j in range(2):
            total = total + rgx[j, l, cc].astype(F32) + rgd[j, cc].astype(F32)
        ot[cc] = total.astype(BF16)
    for copy in sent:
        copy.wait_send()
    for copy in stores:
        copy.wait()
    assert len(sent) <= N_REMOTE


def copy_kernel(gt_in, dwg_in, dwu_in, dwd_in, gt_out, dwg_out, dwu_out, dwd_out, held_g, held_d, sems):
    reads = [
        pltpu.make_async_copy(dwg_in, held_g, sems.at[0]),
        pltpu.make_async_copy(dwd_in, held_d, sems.at[1]),
    ]
    writes = [
        pltpu.make_async_copy(held_g, dwg_out, sems.at[2]),
        pltpu.make_async_copy(held_d, dwd_out, sems.at[3]),
        pltpu.make_async_copy(gt_in, gt_out, sems.at[4]),
        pltpu.make_async_copy(dwu_in, dwu_out, sems.at[5]),
    ]
    for copy in reads + writes[2:]:
        copy.start()
    for read, write in zip(reads, writes):
        read.wait()
        write.start()
    for copy in writes:
        copy.wait()


def local_step(tokens, grad_out, gate_pre, up_pre, gate_weight, up_weight, down_weight):
    any_spec = pl.BlockSpec(memory_space=pl.ANY)
    vm = pltpu.VMEM
    vm_spec = pl.BlockSpec(memory_space=vm)
    outs = pl.pallas_call(
        kernel,
        out_shape=(
            vm((2, 2, 32, DB), BF16),
            jax.ShapeDtypeStruct((FB, DB), BF16),
            vm((FB, DB), BF16),
            jax.ShapeDtypeStruct((FB, DB), BF16),
        ),
        in_specs=[any_spec] * 7,
        out_specs=(vm_spec, any_spec, vm_spec, any_spec),
        scratch_shapes=[
            vm((2, 2, 2, 4, 2, 32, FB), BF16),
            vm((2, 2, 4, 2, 32, FB), BF16),
            vm((2, 2, 2, 4, 2, 32, FB), BF16),
            vm((2, 2, 4, 2, 32, FB), BF16),
            vm((2, 2, 8, 32, DB), BF16),
            vm((2, 2, 8, 32, DB), BF16),
            vm((2, 8, 32, DB), BF16),
            vm((FB, DB), BF16),
            vm((FB, DB), BF16),
            vm((FB, DB), BF16),
            vm((FB, DB), BF16),
            vm((4, 2, 2, 32, FB), BF16),
            vm((4, 3, 32, FB), BF16),
            vm((4, 32, FB), BF16),
            vm((4, 16, FB), BF16),
            vm((4, 2, 2, 16, FB), BF16),
            vm((4, 2, 2, 16, FB), BF16),
            vm((4, 3, 16, FB), BF16),
            vm((4, 7, 16, FB), BF16),
            vm((4, 2, 2, 2, 32, DB), BF16),
            vm((2, 2, 2, 2, 32, DB), BF16),
            vm((2, 2, 2, 32, DB), BF16),
            vm((2, 2, 32, DB), BF16),
            vm((2, 2, 32, DB), BF16),
            vm((FB, DB), BF16),
            vm((FB, DB), BF16),
            pltpu.SemaphoreType.DMA((N_REMOTE,)),
            pltpu.SemaphoreType.DMA((N_REMOTE,)),
            pltpu.SemaphoreType.DMA((16,)),
        ],
        compiler_params=pltpu.CompilerParams(
            collective_id=0, has_side_effects=True, vmem_limit_bytes=60 * 1024 * 1024
        ),
        name="swiglu_backward",
    )(
        tokens.reshape(2, 2, 32, DB),
        grad_out.reshape(2, 2, 32, DB),
        gate_pre.reshape(2, 32, FB),
        up_pre.reshape(2, 32, FB),
        gate_weight.T,
        up_weight.T,
        down_weight,
    )
    outs = pl.pallas_call(
        copy_kernel,
        out_shape=tuple(jax.ShapeDtypeStruct(o.shape, o.dtype) for o in outs),
        in_specs=[vm_spec, any_spec, vm_spec, any_spec],
        out_specs=(any_spec,) * 4,
        scratch_shapes=[vm((FB, DB), BF16)] * 2 + [pltpu.SemaphoreType.DMA((6,))],
        name="hand_out",
    )(
        pltpu.with_memory_space_constraint(outs[0], vm),
        outs[1],
        pltpu.with_memory_space_constraint(outs[2], vm),
        outs[3],
    )
    return (outs[0].reshape(128, DB), outs[1].T, outs[2].T, outs[3])


def solution(mesh):
    return jax.shard_map(
        local_step,
        mesh=mesh,
        in_specs=(
            P("gy", ("gx", "gz")),
            P("gy", ("gx", "gz")),
            P(("gx", "gz"), "gy"),
            P(("gx", "gz"), "gy"),
            P(("gx", "gz"), "gy"),
            P(("gx", "gz"), "gy"),
            P("gy", ("gx", "gz")),
        ),
        out_specs=(
            P("gy", ("gx", "gz")),
            P(("gx", "gz"), "gy"),
            P(("gx", "gz"), "gy"),
            P("gy", ("gx", "gz")),
        ),
        check_vma=False,
    )
```

time: 115 us -> 99.2 us (0.86)
  local copies, waits for them, and re-layouts: 16.5 us -> 0 us
    unnamed x12 -> x0, local copies, waits for them, and re-layouts: 16.5 us -> none
    pallas_call x1 -> x2, Pallas kernels: 97.4 us -> 97.2 us  [the longest x1 93 us: local_step(): pl.pallas_call(kernel, out_shape=(vm((2, 2, 32, DB), BF16), jax.ShapeDtyp...]
where the time goes in v2:
time: 99.2 us; the launch traced here: 98 us
  Pallas kernels  97.2 us (98%)
    pallas_call x1, Pallas kernels, local_step(): pl.pallas_call(kernel, out_shape=(vm((2, 2, 32, DB), BF16), jax.ShapeDtyp...  93 us
    pallas_call x1, Pallas kernels, local_step(): pl.pallas_call(copy_kernel, out_shape=tuple((jax.ShapeDtypeStruct(o.shape...  4.18 us

profile of v2, /device:TPU:1, one launch (start us, length us, event | category | flops | bytes accessed | tf_op | source)
XLA Modules:
  0.0 98.0 jit_solution(7752864830584902164)
XLA Ops:
  0.6 93.0 %swiglu_backward.1 = (bf16[2,2,32,512]{3,2,1,0:T(8,128)(2,1)S(1)}, bf16[1848,512]{1,0:T(8,128)(2,1)}, bf16[1848,512]{1,0:T(8,128)(2,1)S(1)}, bf16[1848,512]{1,0:T(8,128)(2,1)}) custom-call(bf16[2,2,32,512]{3,2,1,0:T(8,128)(2,1)} %bitcast.13, bf16[2,2,32,512]{3,2,1,0:T(8,128)(2,1)} %bitcast.14, bf16[2,32,1848]{2,1,0:T(8,128)(2,1)} %bitcast.11, ...), custom_call_target="tpu_custom_call" | custom-call | tf_op jit(solution)/shard_map/swiglu_backward/pallas_call | solution.py:382
  93.6 4.2 %hand_out.1 = (bf16[2,2,32,512]{3,2,1,0:T(8,128)(2,1)}, bf16[1848,512]{1,0:T(8,128)(2,1)}, bf16[1848,512]{1,0:T(8,128)(2,1)}, bf16[1848,512]{1,0:T(8,128)(2,1)}) custom-call(bf16[2,2,32,512]{3,2,1,0:T(8,128)(2,1)S(1)} %get-tuple-element.12.gt_in, bf16[1848,512]{1,0:T(8,128)(2,1)} %get-tuple-element.13.dwg_in, ...), custom_call_target="tpu_custom_call" | custom-call | tf_op jit(solution)/shard_map/hand_out/pallas_call | solution.py:436

commit v3 on v2

--- a/solution.py
+++ b/solution.py
@@ -15,8 +15,7 @@
 DB = 512
 LANES = ((0, 512), (512, 1024), (1024, 1536), (1536, 1848))
 N_REMOTE = 112
-CHIPS = ((1, 0), (3, 0), (0, 1), (2, 0), (1, 1), (3, 1), (2, 1))
-ORDER = ((0, "y"), (1, "z"), (3, "y"), (2, "z"))
+ORDER = ((1, "y"), (0, "z"), (3, "z"), (2, "y"))
 SCALE = 1.0 / 32.0
 
 
@@ -35,7 +34,7 @@
 def kernel(
     tok_in, go_in, gate_in, up_in, wg_in, wu_in, dw_in,
     ot, dwg_out, ou, dwd_out,
-    gu, hg, ab, hid, go, tok, gos, dw, dws, wg, wu, part, r1, s1, r2, r3, q1, r4, r5,
+    gu, hg, ab, hid, go, tok, gos, dw, dws, wg, wu, part, r1, s1, r2, r3, q1, r4,
     gt, rgx, rgd, sl, rl, og, od, ss, rs, ls,
 ):
     z = lax.axis_index("gx")
@@ -52,9 +51,6 @@
 
     hidev = (z, gy, nh * 2 + c)
     sib = (z, gy, h * 2 + nc)
-
-    def chip(e, f):
-        return (zs[e], gy, (nh if f else h) * 2 + c)
 
     def gydev(dx, dl):
         return (z, lax.rem(x + dx, 4) * 2 + lax.rem(l + dl, 2), gz)
@@ -138,18 +134,11 @@
             part[xt, :, :, :, a:b] = p.astype(BF16).reshape(2, 2, 32, b - a)
         if kind[d] == "z":
             one[d] = [send(part.at[xt, zk[e], zh[e]], r1.at[slot[d], e - 1], zdev(e)) for e in (1, 3, 2)]
-        elif kind[d] == "d":
-            one[d] = [
-                send(part.at[xt, zk[e], zh[e], (mine, theirs)[f]], r5.at[slot[d], j], chip(e, f))
-                for j, (e, f) in enumerate(CHIPS)
-            ]
         else:
             one[d] = [send(part.at[xt, :, :, theirs], r3.at[slot[d]], hidev)]
 
     def middle(d):
         xt, i = xts[d], slot[d]
-        if kind[d] == "d":
-            return
         for copy in one[d]:
             copy.wait_recv()
         if kind[d] == "z":
@@ -167,15 +156,11 @@
 
     def own_sum(d):
         xt, i = xts[d], slot[d]
-        for copy in one[d] if kind[d] == "d" else two[d]:
+        for copy in two[d]:
             copy.wait_recv()
         for a, b in LANES:
             if kind[d] == "z":
                 total = s1[i, mine, a:b].astype(F32) + r2[i, :, a:b].astype(F32)
-            elif kind[d] == "d":
-                total = part[xt, zk[0], zh[0], mine, a:b].astype(F32)
-                for j in range(7):
-                    total = total + r5[i, j, :, a:b].astype(F32)
             else:
                 total = q1[i, zk[0], zh[0], :, a:b].astype(F32)
                 for e in range(3):
@@ -184,16 +169,12 @@
         block = hg.at[c, zk[0], xt, zh[0], mine]
         if kind[d] == "z":
             spread_one[d] = [same(block, hidev)]
-        elif kind[d] == "d":
-            spread_one[d] = [same(block, chip(e, f)) for e, f in CHIPS]
         else:
             spread_one[d] = [same(block, zdev(e)) for e in (1, 2, 3)]
             spread_two[d] = [same(block, hidev)]
 
     def spread(d):
         xt = xts[d]
-        if kind[d] == "d":
-            return
         if kind[d] == "z":
             spread_one[d][0].wait_recv()
             pair = hg.at[c, zk[0], xt, zh[0]]
@@ -211,10 +192,6 @@
             for e in (1, 2, 3):
                 spread_two[d][e - 1].wait_recv()
                 to_sib[d].append(same(hg.at[c, zk[4 - e], xt, zh[4 - e]], sib))
-        elif kind[d] == "d":
-            for copy in spread_one[d]:
-                copy.wait_recv()
-            to_sib[d] = [same(hg.at[c, :, xt], sib)]
         else:
             for copy in spread_two[d]:
                 copy.wait_recv()
@@ -245,7 +222,7 @@
         elif d:
             gt_copies.append(send(gt.at[xt], rgx.at[len(gt_copies)], (z, xt * 2 + l, gz)))
 
-    def pointwise(cc, k):
+    def pointwise(cc, k, part_of):
         def block(i, carry):
             zz, hh = i // 2, i % 2
             for a, b in LANES:
@@ -258,81 +235,119 @@
                 hid[cc, k, zz, hh, :, a:b] = (silu * up).astype(BF16)
             return carry
 
-        lax.fori_loop(0, 8, block, 0)
-
-    d0, d1, d2, d3 = [d for d, _ in ORDER]
-    product(d0)
-    gu1_z[0].wait_recv()
-    gu1_f = [same(gu.at[0, c, 1, zs[3], h], zdev(1))]
-    gu1_z[1].wait_recv()
-    gu1_f.append(same(gu.at[1, c, 1, zs[1], h], zdev(3)))
-    gu0_hi.wait_recv()
-    gu0_z = [same(gu.at[:, c, 0, z], zdev(d)) for d in (1, 3)]
-    product(d1)
-    gu1_hi += [same(gu.at[:, c, 1, zs[d], h], hidev) for d in (1, 3)]
-    product(d2)
-    middle(d0)
-    product(d3)
-    middle(d1)
-    l_tok.wait()
-    tok_lo = same(tok.at[:, :, gy], gydev(0, 1))
-    tok_x = [same(tok.at[:, :, gy], gydev(d, 0)) for d in (1, 2, 3)]
-    own_sum(d0)
-    middle(d2)
-    for copy in gu1_f:
-        copy.wait_recv()
-    gu1_hi.append(same(gu.at[:, c, 1, zs[2], h], hidev))
-    gu1_s = same(gu.at[:, c, 1, :, h], sib)
-    own_sum(d1)
-    spread(d0)
-    middle(d3)
-    gu0_z[0].wait_recv()
-    gu0_f = [same(gu.at[0, c, 0, zs[3]], zdev(1))]
-    gu0_z[1].wait_recv()
-    gu0_f.append(same(gu.at[1, c, 0, zs[1]], zdev(3)))
-    own_sum(d2)
-    spread(d1)
-    tok_lo.wait_recv()
-    tok_x2 = [same(tok.at[:, :, other_gy], gydev(d, 0)) for d in (1, 2, 3)]
-    last_spread(d0)
-    own_sum(d3)
-    spread(d2)
-    for copy in gu1_hi:
-        copy.wait_recv()
-    gu1_s2 = same(gu.at[:, c, 1, :, nh], sib)
-    pointwise(c, 1)
-    last_spread(d1)
-    spread(d3)
-    for copy in gu0_f:
-        copy.wait_recv()
-    gu0_s = same(gu.at[:, c, 0], sib)
-    pointwise(c, 0)
-    gu1_s.wait_recv()
-    gu1_s2.wait_recv()
-    pointwise(nc, 1)
-    last_spread(d2)
-    gu0_s.wait_recv()
-    pointwise(nc, 0)
+        lax.fori_loop(4 * part_of, 4 * part_of + 4, block, 0)
+
+    gu1_f, gu0_z, gu0_f, gu_s, tok_lo, tok_x, lo_sum, stores = [], [], [], {}, [], [], [], []
+
+    def gate_up_1():
+        gu1_z[0].wait_recv()
+        gu1_f.append(same(gu.at[0, c, 1, zs[3], h], zdev(1)))
+        gu1_z[1].wait_recv()
+        gu1_f.append(same(gu.at[1, c, 1, zs[1], h], zdev(3)))
+
+    def gate_up_2():
+        gu0_hi.wait_recv()
+        gu0_z.extend([same(gu.at[:, c, 0, z], zdev(d)) for d in (1, 3)])
+
+    def gate_up_3():
+        gu1_hi.extend([same(gu.at[:, c, 1, zs[d], h], hidev) for d in (1, 3)])
+
+    def gate_up_4():
+        for copy in gu1_f:
+            copy.wait_recv()
+        gu1_hi.append(same(gu.at[:, c, 1, zs[2], h], hidev))
+        gu_s[0] = same(gu.at[:, c, 1, :, h], sib)
+
+    def gate_up_5():
+        gu0_z[0].wait_recv()
+        gu0_f.append(same(gu.at[0, c, 0, zs[3]], zdev(1)))
+        gu0_z[1].wait_recv()
+        gu0_f.append(same(gu.at[1, c, 0, zs[1]], zdev(3)))
+
+    def gate_up_6():
+        for copy in gu1_hi:
+            copy.wait_recv()
+        gu_s[1] = same(gu.at[:, c, 1, :, nh], sib)
+
+    def gate_up_7():
+        for copy in gu0_f:
+            copy.wait_recv()
+        gu_s[2] = same(gu.at[:, c, 0], sib)
+
+    def tokens_1():
+        l_tok.wait()
+        tok_lo.append(same(tok.at[:, :, gy], gydev(0, 1)))
+        tok_x.extend([same(tok.at[:, :, gy], gydev(d, 0)) for d in (1, 2, 3)])
+
+    def tokens_2():
+        tok_lo[0].wait_recv()
+        tok_x.extend([same(tok.at[:, :, other_gy], gydev(d, 0)) for d in (1, 2, 3)])
+
+    def sum_lo():
+        for copy in gt_copies:
+            copy.wait_recv()
+        for cc in range(2):
+            total = gt[x, 1 - l, cc].astype(F32) + rgx[0, 1 - l, cc].astype(F32) + rgx[1, 1 - l, cc].astype(F32)
+            sl[cc] = total.astype(BF16)
+        gt_last.append(send(sl, rl, gydev(0, 1)))
+
+    def down_grad():
+        for a, b in LANES:
+            w = tn(hid[:, :, :, :, :, a:b].reshape(1024, b - a), go[...].reshape(1024, DB))
+            od[a:b, :] = (w * SCALE).astype(BF16)
+        stores.append(local(od, dwd_out))
+
+    gate_up_1()
+    gate_up_3()
+    product(0)
+    gate_up_2()
+    middle(0)
+    product(3)
+    gate_up_4()
+    gu_s[0].wait_recv()
+    product(1)
+    product(2)
+    gate_up_6()
+    gate_up_5()
+    middle(3)
+    middle(1)
+    own_sum(3)
+    gu_s[1].wait_recv()
+    gate_up_7()
+    pointwise(nc, 1, 1)
+    middle(2)
+    pointwise(c, 1, 0)
+    tokens_1()
+    pointwise(nc, 1, 0)
+    own_sum(1)
+    gu_s[2].wait_recv()
+    pointwise(c, 0, 1)
+    pointwise(c, 0, 0)
+    spread(3)
+    own_sum(0)
+    pointwise(nc, 0, 0)
+    spread(1)
+    pointwise(nc, 0, 1)
+    own_sum(2)
+    pointwise(c, 1, 1)
+    tokens_2()
+    down_grad()
+    last_spread(3)
+    last_spread(1)
+    spread(0)
+    spread(2)
     l_wg.wait()
     l_wu.wait()
-    input_grad(d0)
-    last_spread(d3)
-    input_grad(d1)
-    input_grad(d2)
-    input_grad(d3)
-    for copy in gt_copies:
+    input_grad(3)
+    input_grad(1)
+    last_spread(2)
+    last_spread(0)
+    input_grad(2)
+    input_grad(0)
+    sum_lo()
+    for copy in tok_x:
         copy.wait_recv()
-    for cc in range(2):
-        total = gt[x, 1 - l, cc].astype(F32) + rgx[0, 1 - l, cc].astype(F32) + rgx[1, 1 - l, cc].astype(F32)
-        sl[cc] = total.astype(BF16)
-    gt_last.append(send(sl, rl, gydev(0, 1)))
-    for copy in tok_x + tok_x2:
-        copy.wait_recv()
-    stores = []
-    for a, b in LANES:
-        w = tn(hid[:, :, :, :, :, a:b].reshape(1024, b - a), go[...].reshape(1024, DB))
-        od[a:b, :] = (w * SCALE).astype(BF16)
-    stores.append(local(od, dwd_out))
+
     for which, out in enumerate((og, ou)):
         for a, b in LANES:
             grads = ab[which, :, :, :, :, :, a:b].reshape(1024, b - a)
@@ -408,7 +423,6 @@
             vm((4, 2, 2, 16, FB), BF16),
             vm((4, 2, 2, 16, FB), BF16),
             vm((4, 3, 16, FB), BF16),
-            vm((4, 7, 16, FB), BF16),
             vm((4, 2, 2, 2, 32, DB), BF16),
             vm((2, 2, 2, 2, 32, DB), BF16),
             vm((2, 2, 2, 32, DB), BF16),

time: 99.2 us -> 92.8 us (0.935)
  Pallas kernels: 97.2 us -> 90.9 us
    pallas_call x1, Pallas kernels: 93 us -> 86.7 us  [local_step(): pl.pallas_call(kernel, out_shape=(vm((2, 2, 32, DB), BF16), jax.ShapeDtyp...]
where the time goes in v3:
time: 92.8 us; the launch traced here: 91.7 us
  Pallas kernels  90.9 us (98%)
    pallas_call x1, Pallas kernels, local_step(): pl.pallas_call(kernel, out_shape=(vm((2, 2, 32, DB), BF16), jax.ShapeDtyp...  86.7 us
    pallas_call x1, Pallas kernels, local_step(): pl.pallas_call(copy_kernel, out_shape=tuple((jax.ShapeDtypeStruct(o.shape...  4.18 us

profile of v3, /device:TPU:1, one launch (start us, length us, event | category | flops | bytes accessed | tf_op | source)
XLA Modules:
  0.0 91.7 jit_solution(18430790563628998548)
XLA Ops:
  0.6 86.7 %swiglu_backward.1 = (bf16[2,2,32,512]{3,2,1,0:T(8,128)(2,1)S(1)}, bf16[1848,512]{1,0:T(8,128)(2,1)}, bf16[1848,512]{1,0:T(8,128)(2,1)S(1)}, bf16[1848,512]{1,0:T(8,128)(2,1)}) custom-call(bf16[2,2,32,512]{3,2,1,0:T(8,128)(2,1)} %bitcast.13, bf16[2,2,32,512]{3,2,1,0:T(8,128)(2,1)} %bitcast.14, bf16[2,32,1848]{2,1,0:T(8,128)(2,1)} %bitcast.11, ...), custom_call_target="tpu_custom_call" | custom-call | tf_op jit(solution)/shard_map/swiglu_backward/pallas_call | solution.py:397
  87.4 4.2 %hand_out.1 = (bf16[2,2,32,512]{3,2,1,0:T(8,128)(2,1)}, bf16[1848,512]{1,0:T(8,128)(2,1)}, bf16[1848,512]{1,0:T(8,128)(2,1)}, bf16[1848,512]{1,0:T(8,128)(2,1)}) custom-call(bf16[2,2,32,512]{3,2,1,0:T(8,128)(2,1)S(1)} %get-tuple-element.12.gt_in, bf16[1848,512]{1,0:T(8,128)(2,1)} %get-tuple-element.13.dwg_in, ...), custom_call_target="tpu_custom_call" | custom-call | tf_op jit(solution)/shard_map/hand_out/pallas_call | solution.py:450

commit v4 on v3

--- a/solution.py
+++ b/solution.py
@@ -15,7 +15,7 @@
 DB = 512
 LANES = ((0, 512), (512, 1024), (1024, 1536), (1536, 1848))
 N_REMOTE = 112
-ORDER = ((1, "y"), (0, "z"), (3, "z"), (2, "y"))
+ORDER = ((1, "y"), (3, "z"), (0, "z"), (2, "y"))
 SCALE = 1.0 / 32.0
 
 
@@ -103,11 +103,20 @@
     c_dws = send(dw, dws, sib)
     l_gate.wait()
     l_up.wait()
-    gu1_z = [same(gu.at[:, c, 1, z, h], zdev(d)) for d in (1, 3)]
-    gu0_hi = same(gu.at[:, c, 0, z, h], hidev)
-    gu1_hi = [same(gu.at[:, c, 1, z, h], hidev)]
-    go_lo.wait_recv()
-    go_other = {d: same(go.at[:, :, other_gy], gydev(d, 0)) for d in (1, 3, 2)}
+    go_other, gu1_z, gu0_hi, gu1_hi = {}, [], [], []
+
+    def grad_out_2():
+        go_lo.wait_recv()
+        go_other.update({d: same(go.at[:, :, other_gy], gydev(d, 0)) for d in (1, 3, 2)})
+
+    def gate_up_z():
+        gu1_z.extend([same(gu.at[:, c, 1, z, h], zdev(d)) for d in (1, 3)])
+
+    def gate_up_y0():
+        gu0_hi.append(same(gu.at[:, c, 0, z, h], hidev))
+
+    def gate_up_y1():
+        gu1_hi.append(same(gu.at[:, c, 1, z, h], hidev))
 
     xts = {d: lax.rem(x + (4 - d), 4) for d in range(4)}
     kind = dict(ORDER)
@@ -124,8 +133,6 @@
             go_own[d].wait_recv()
             go_other[d].wait_recv()
         gos_d = send(go.at[nc, :, pair], gos.at[:, pair], sib)
-        if not d:
-            c_dws.wait_recv()
         gos_d.wait_recv()
         own = go[c, :, pair].reshape(128, DB)
         other = gos[:, pair].reshape(128, DB)
@@ -246,7 +253,7 @@
         gu1_f.append(same(gu.at[1, c, 1, zs[1], h], zdev(3)))
 
     def gate_up_2():
-        gu0_hi.wait_recv()
+        gu0_hi[0].wait_recv()
         gu0_z.extend([same(gu.at[:, c, 0, z], zdev(d)) for d in (1, 3)])
 
     def gate_up_3():
@@ -297,54 +304,59 @@
             od[a:b, :] = (w * SCALE).astype(BF16)
         stores.append(local(od, dwd_out))
 
+    gate_up_z()
+    gate_up_y0()
     gate_up_1()
     gate_up_3()
-    product(0)
+    grad_out_2()
     gate_up_2()
-    middle(0)
+    gate_up_4()
+    c_dws.wait_recv()
+    product(1)
     product(3)
-    gate_up_4()
-    gu_s[0].wait_recv()
-    product(1)
+    gate_up_5()
+    gate_up_y1()
     product(2)
-    gate_up_6()
-    gate_up_5()
     middle(3)
     middle(1)
+    product(0)
+    own_sum(1)
+    gu_s[0].wait_recv()
+    gate_up_7()
     own_sum(3)
+    gate_up_6()
+    tokens_1()
+    pointwise(c, 0, 1)
+    middle(2)
+    middle(0)
+    pointwise(c, 1, 0)
+    gu_s[2].wait_recv()
     gu_s[1].wait_recv()
-    gate_up_7()
+    spread(1)
+    spread(3)
+    pointwise(nc, 0, 1)
+    pointwise(c, 1, 1)
+    own_sum(0)
     pointwise(nc, 1, 1)
-    middle(2)
-    pointwise(c, 1, 0)
-    tokens_1()
+    own_sum(2)
     pointwise(nc, 1, 0)
-    own_sum(1)
-    gu_s[2].wait_recv()
-    pointwise(c, 0, 1)
     pointwise(c, 0, 0)
-    spread(3)
-    own_sum(0)
+    tokens_2()
+    spread(0)
+    last_spread(1)
     pointwise(nc, 0, 0)
-    spread(1)
-    pointwise(nc, 0, 1)
-    own_sum(2)
-    pointwise(c, 1, 1)
-    tokens_2()
-    down_grad()
     last_spread(3)
-    last_spread(1)
-    spread(0)
     spread(2)
     l_wg.wait()
     l_wu.wait()
+    input_grad(1)
     input_grad(3)
-    input_grad(1)
+    last_spread(0)
     last_spread(2)
-    last_spread(0)
     input_grad(2)
     input_grad(0)
     sum_lo()
+    down_grad()
     for copy in tok_x:
         copy.wait_recv()
 

time: 92.8 us -> 90.5 us (0.975); the launches traced: 91.7 us -> 90.4 us
  Pallas kernels: 90.9 us -> 89.6 us
    pallas_call x1, Pallas kernels: 86.7 us -> 85.4 us  [local_step(): pl.pallas_call(kernel, out_shape=(vm((2, 2, 32, DB), BF16), jax.ShapeDtyp...]
where the time goes in v4:
time: 90.5 us; the launch traced here: 90.4 us
  Pallas kernels  89.6 us (99%)
    pallas_call x1, Pallas kernels, local_step(): pl.pallas_call(kernel, out_shape=(vm((2, 2, 32, DB), BF16), jax.ShapeDtyp...  85.4 us
    pallas_call x1, Pallas kernels, local_step(): pl.pallas_call(copy_kernel, out_shape=tuple((jax.ShapeDtypeStruct(o.shape...  4.18 us

profile of v4, /device:TPU:1, one launch (start us, length us, event | category | flops | bytes accessed | tf_op | source)
XLA Modules:
  0.0 90.4 jit_solution(7749917556514595504)
XLA Ops:
  0.6 85.4 %swiglu_backward.1 = (bf16[2,2,32,512]{3,2,1,0:T(8,128)(2,1)S(1)}, bf16[1848,512]{1,0:T(8,128)(2,1)}, bf16[1848,512]{1,0:T(8,128)(2,1)S(1)}, bf16[1848,512]{1,0:T(8,128)(2,1)}) custom-call(bf16[2,2,32,512]{3,2,1,0:T(8,128)(2,1)} %bitcast.13, bf16[2,2,32,512]{3,2,1,0:T(8,128)(2,1)} %bitcast.14, bf16[2,32,1848]{2,1,0:T(8,128)(2,1)} %bitcast.11, ...), custom_call_target="tpu_custom_call" | custom-call | tf_op jit(solution)/shard_map/swiglu_backward/pallas_call | solution.py:409
  86.0 4.2 %hand_out.1 = (bf16[2,2,32,512]{3,2,1,0:T(8,128)(2,1)}, bf16[1848,512]{1,0:T(8,128)(2,1)}, bf16[1848,512]{1,0:T(8,128)(2,1)}, bf16[1848,512]{1,0:T(8,128)(2,1)}) custom-call(bf16[2,2,32,512]{3,2,1,0:T(8,128)(2,1)S(1)} %get-tuple-element.12.gt_in, bf16[1848,512]{1,0:T(8,128)(2,1)} %get-tuple-element.13.dwg_in, ...), custom_call_target="tpu_custom_call" | custom-call | tf_op jit(solution)/shard_map/hand_out/pallas_call | solution.py:462
